TPU v7x, 1024 devices: a whole 8x8x8 slice. The times are simulated.
1024 devices in a mesh: group: 4 (over y_hi), blk: 256 (over z, y_lo, x, core).
Axes of the slice: x: 8, y: 8 (y_hi: 4, y_lo: 2; y = y_hi * 2 + y_lo), z: 8, core: 2. Of those that a mesh axis runs over, the one named last changes fastest.
Arguments:
- image_emb: bfloat16 [262144, 1152], P(('group', 'blk')), may hold values from -4 to 4
- text_emb: bfloat16 [262144, 1152], P(('group', 'blk')), may hold values from -4 to 4
- image_ids: int32 [262144], P(('group', 'blk')), may hold values from 0 to 127
- text_ids: int32 [262144], P(('group', 'blk')), may hold values from 0 to 127
Outputs:
- row_loss: float32 [262144], P(('group', 'blk'))
- image_grad: bfloat16 [262144, 1152], P(('group', 'blk'))
- text_grad: bfloat16 [262144, 1152], P(('group', 'blk'))
All inputs are finite; a program needn't handle non-finite values.
Results may differ from a plain program's by a relative error of at most 0.0077.
Values may be sent and summed in bfloat16 or wider, within the bound.
A program may use at most 32 MiB of HBM per device.

v0:
```python
import jax
import jax.numpy as jnp
from jax import lax
from jax.sharding import PartitionSpec as P

logit_scale = 10.0
logit_bias = -3.0


def passed_along(value, axis, steps):
    count = lax.axis_size(axis)
    pairs = [(source, (source + steps) % count) for source in range(count)]
    return lax.ppermute(value, axis, pairs)


def signed_logits(images, image_tags, texts, text_tags):
    scores = lax.dot_general(
        images, texts, (((1,), (1,)), ((), ())), preferred_element_type=jnp.float32
    )
    logits = logit_scale * scores + logit_bias
    matched = image_tags.astype(jnp.float32)[:, None] == text_tags.astype(jnp.float32)[None, :]
    pair_sign = jnp.where(matched, 1.0, -1.0).astype(jnp.float32)
    return (-pair_sign * logits, pair_sign)


def loss_terms(signed):
    return jnp.sum(jax.nn.softplus(signed), axis=1)


def slope_block(signed, pair_sign):
    return (-pair_sign * jax.nn.sigmoid(signed)).astype(jnp.bfloat16)


def image_side(slopes, texts):
    return logit_scale * jnp.dot(slopes, texts, preferred_element_type=jnp.float32)


def text_side(slopes, images):
    return logit_scale * lax.dot_general(
        slopes, images, (((0,), (0,)), ((), ())), preferred_element_type=jnp.float32
    )


def per_device(image_emb, text_emb, image_ids, text_ids):
    row_count = image_emb.shape[0]
    own_tags = text_ids.astype(jnp.bfloat16)
    near_block = passed_along((text_emb, own_tags), "blk", 1)
    far_block = passed_along((near_block[0], near_block[1]), "blk", 1)
    across = passed_along((text_emb, own_tags), "group", 1)
    signed, pair_sign = signed_logits(image_emb, image_ids, text_emb, own_tags)
    slopes = slope_block(signed, pair_sign)
    loss_total = loss_terms(signed)
    image_total = image_side(slopes, text_emb)
    text_total = text_side(slopes, image_emb)
    visitor_slopes = []
    for visitor in (near_block, far_block, across):
        signed, pair_sign = signed_logits(image_emb, image_ids, visitor[0], visitor[1])
        slopes = slope_block(signed, pair_sign)
        loss_total = loss_total + loss_terms(signed)
        image_total = image_total + image_side(slopes, visitor[0])
        visitor_slopes.append(slopes)
    cross_part = text_side(visitor_slopes[2], image_emb)
    near_part = text_side(visitor_slopes[0], image_emb)
    far_part = text_side(visitor_slopes[1], image_emb)
    back_near = passed_along(near_part, "blk", -1)
    back_far = passed_along(far_part, "blk", -2)
    text_total = text_total + back_near + back_far
    text_total = text_total + passed_along(cross_part, "group", -1)
    row_loss = loss_total / (4 * row_count)
    return (row_loss, image_total.astype(jnp.bfloat16), text_total.astype(jnp.bfloat16))


def solution(mesh):
    in_specs = (
        P(("group", "blk"), None),
        P(("group", "blk"), None),
        P(("group", "blk")),
        P(("group", "blk")),
    )
    out_specs = (P(("group", "blk")), P(("group", "blk"), None), P(("group", "blk"), None))
    return jax.shard_map(
        per_device, mesh=mesh, in_specs=in_specs, out_specs=out_specs, check_vma=False
    )
```

profile of v0, /device:TPU:799, one launch (start us, length us, event | category | flops | bytes accessed | tf_op | source)
XLA Modules:
  0.0 136.7 jit_solution(5212480712171824455)
XLA Ops:
  0.6 0.0 copy-start
  0.6 4.3 %collective-permute-start.1 = (bf16[256,1152]{1,0:T(8,128)(2,1)}, bf16[256,1152]{1,0:T(8,128)(2,1)S(1)}, u32[]{:S(2)}, u32[]{:S(2)}) collective-permute-start(bf16[256,1152]{1,0:T(8,128)(2,1)} %param.5), channel_id=1, source_target_pairs={{0,1},{1,2},{2,3},{3,4},{4,5},{5,6},{6,7},{7,8},{8,9},{9,10},{10,1... | collective-permute-start | bytes 1769480 | tf_op jit(solution)/shard_map/ppermute | solution.py:13
  4.9 19.8 %collective-permute-start.5 = (bf16[256,1152]{1,0:T(8,128)(2,1)}, bf16[256,1152]{1,0:T(8,128)(2,1)S(1)}, u32[]{:S(2)}, u32[]{:S(2)}) collective-permute-start(bf16[256,1152]{1,0:T(8,128)(2,1)} %param.5), channel_id=1, source_target_pairs={{0,256},{256,512},{512,768},{768,0},{1,257},{257,513},{513,769},{7... | collective-permute-start | bytes 1769480 | tf_op jit(solution)/shard_map/ppermute | solution.py:13
  24.7 0.7 fusion.21
  25.4 2.2 %collective-permute-start = (bf16[256]{0:T(256)(128)(2,1)S(1)}, bf16[256]{0:T(256)(128)(2,1)S(1)}, u32[]{:S(2)}, u32[]{:S(2)}) collective-permute-start(bf16[256]{0:T(256)(128)(2,1)S(1)} %get-tuple-element.4), channel_id=1, source_target_pairs={{0,1},{1,2},{2,3},{3,4},{4,5},{5,6},{6,7},{7,8},{8,9},{9,10},{10,1... | collective-permute-start | bytes 1544 | tf_op jit(solution)/shard_map/ppermute | solution.py:13
  27.6 5.2 %collective-permute-start.4 = (bf16[256]{0:T(256)(128)(2,1)S(1)}, bf16[256]{0:T(256)(128)(2,1)S(1)}, u32[]{:S(2)}, u32[]{:S(2)}) collective-permute-start(bf16[256]{0:T(256)(128)(2,1)S(1)} %get-tuple-element.4), channel_id=1, source_target_pairs={{0,256},{256,512},{512,768},{768,0},{1,257},{257,513},{513,769},{7... | collective-permute-start | bytes 1544 | tf_op jit(solution)/shard_map/ppermute | solution.py:13
  32.9 0.7 convert_element_type.39
  33.6 0.0 collective-permute-done
  33.6 2.2 %collective-permute-start.2 = (bf16[256]{0:T(256)(128)(2,1)S(1)}, bf16[256]{0:T(256)(128)(2,1)S(1)}, u32[]{:S(2)}, u32[]{:S(2)}) collective-permute-start(bf16[256]{0:T(256)(128)(2,1)S(1)} %collective-permute-done), channel_id=1, source_target_pairs={{0,1},{1,2},{2,3},{3,4},{4,5},{5,6},{6,7},{7,8},{8,9},{9,10},{10,1... | collective-permute-start | bytes 1544 | tf_op jit(solution)/shard_map/ppermute | solution.py:13
  35.8 0.0 copy-done
  35.8 1.6 %fusion.15 = (f32[256]{0:T(256)S(1)}, f32[256,256]{0,1:T(8,128)S(1)}) fusion(bf16[256,1152]{1,0:T(8,128)(2,1)S(1)} %copy-done, bf16[256,1152]{1,0:T(8,128)(2,1)} %param.5, f32[256]{0:T(256)S(1)} %get-tuple-element.3, f32[256]{0:T(256)S(1)} %convert_element_type.39), kind=kOutput, calls=%fused_computation.29 | convolution fusion | flops 151846656 | bytes 1444864 | tf_op jit(solution)/shard_map/dot_general | solution.py:17
  37.4 0.0 collective-permute-done.4
  37.4 0.0 collective-permute-done.2
  37.4 0.0 collective-permute-done.1
  37.4 21.2 %collective-permute-start.3 = (bf16[256,1152]{1,0:T(8,128)(2,1)S(1)}, bf16[256,1152]{1,0:T(8,128)(2,1)S(1)}, u32[]{:S(2)}, u32[]{:S(2)}) collective-permute-start(bf16[256,1152]{1,0:T(8,128)(2,1)S(1)} %collective-permute-done.1), channel_id=1, source_target_pairs={{0,1},{1,2},{2,3},{3,4},{4,5},{5,6},{6,7},{7,8},{8,9},{9,10},{10,1... | collective-permute-start | bytes 1769480 | tf_op jit(solution)/shard_map/ppermute | solution.py:13
  58.6 0.0 collective-permute-done.5
  58.6 0.5 fusion.18
  59.1 0.4 convolution_multiply_fusion
  59.6 6.2 %collective-permute-start.8 = (f32[256,1152]{1,0:T(8,128)S(1)}, f32[256,1152]{1,0:T(8,128)S(1)}, u32[]{:S(2)}, u32[]{:S(2)}) collective-permute-start(f32[256,1152]{1,0:T(8,128)S(1)} %convolution_multiply_fusion), channel_id=1, source_target_pairs={{0,768},{256,0},{512,256},{768,512},{1,769},{257,1},{513,257},{769... | collective-permute-start | bytes 3538952 | tf_op jit(solution)/shard_map/ppermute | solution.py:13
  65.7 0.5 fusion.16
  66.3 0.4 convolution_multiply_fusion.2
  66.7 1.9 %collective-permute-start.6 = (f32[256,1152]{1,0:T(8,128)S(1)}, f32[256,1152]{1,0:T(8,128)S(1)}, u32[]{:S(2)}, u32[]{:S(2)}) collective-permute-start(f32[256,1152]{1,0:T(8,128)S(1)} %convolution_multiply_fusion.2), channel_id=1, source_target_pairs={{0,255},{1,0},{2,1},{3,2},{4,3},{5,4},{6,5},{7,6},{8,7},{9,8},{10,... | collective-permute-start | bytes 3538952 | tf_op jit(solution)/shard_map/ppermute | solution.py:13
  68.6 0.0 collective-permute-done.3
  68.6 0.5 fusion.17
  69.1 0.0 copy-start.1
  69.2 0.4 convolution_multiply_fusion.1
  69.6 1.9 %collective-permute-start.7 = (f32[256,1152]{1,0:T(8,128)S(1)}, f32[256,1152]{1,0:T(8,128)S(1)}, u32[]{:S(2)}, u32[]{:S(2)}) collective-permute-start(f32[256,1152]{1,0:T(8,128)S(1)} %convolution_multiply_fusion.1), channel_id=1, source_target_pairs={{0,254},{1,255},{2,0},{3,1},{4,2},{5,3},{6,4},{7,5},{8,6},{9,7},{1... | collective-permute-start | bytes 3538952 | tf_op jit(solution)/shard_map/ppermute | solution.py:13
  71.5 0.0 copy-done.1
  71.5 0.5 fusion.19
  72.0 0.5 fusion.20
  72.4 0.5 convolution_add_fusion.1
  72.9 0.6 add_multiply_fusion
  73.4 1.3 fusion.6
  74.7 60.7 %collective-permute-done.8 = f32[256,1152]{1,0:T(8,128)S(1)} collective-permute-done((f32[256,1152]{1,0:T(8,128)S(1)}, f32[256,1152]{1,0:T(8,128)S(1)}, u32[]{:S(2)}, u32[]{:S(2)}) %collective-permute-start.8) | collective-permute-done | bytes 1179680 | tf_op jit(solution)/shard_map/ppermute | solution.py:13
  135.4 0.0 collective-permute-done.6
  135.4 0.0 collective-permute-done.7
  135.4 1.2 fusion.5
  (3 shorter events, 0.0 us)
Async XLA Ops:
  0.6 35.1 %copy-start = (bf16[256,1152]{1,0:T(8,128)(2,1)S(1)}, bf16[256,1152]{1,0:T(8,128)(2,1)}, u32[]{:S(2)}) copy-start(bf16[256,1152]{1,0:T(8,128)(2,1)} %param.4) | copy-start | bytes 1769476
  0.6 36.8 %collective-permute-start.1 = (bf16[256,1152]{1,0:T(8,128)(2,1)}, bf16[256,1152]{1,0:T(8,128)(2,1)S(1)}, u32[]{:S(2)}, u32[]{:S(2)}) collective-permute-start(bf16[256,1152]{1,0:T(8,128)(2,1)} %param.5), channel_id=1, source_target_pairs={{0,1},{1,2},{2,3},{3,4},{4,5},{5,6},{6,7},{7,8},{8,9},{9,10},{10,1... | collective-permute-start | bytes 1769480 | tf_op jit(solution)/shard_map/ppermute | solution.py:13
  4.9 53.7 %collective-permute-start.5 = (bf16[256,1152]{1,0:T(8,128)(2,1)}, bf16[256,1152]{1,0:T(8,128)(2,1)S(1)}, u32[]{:S(2)}, u32[]{:S(2)}) collective-permute-start(bf16[256,1152]{1,0:T(8,128)(2,1)} %param.5), channel_id=1, source_target_pairs={{0,256},{256,512},{512,768},{768,0},{1,257},{257,513},{513,769},{7... | collective-permute-start | bytes 1769480 | tf_op jit(solution)/shard_map/ppermute | solution.py:13
  25.4 8.1 %collective-permute-start = (bf16[256]{0:T(256)(128)(2,1)S(1)}, bf16[256]{0:T(256)(128)(2,1)S(1)}, u32[]{:S(2)}, u32[]{:S(2)}) collective-permute-start(bf16[256]{0:T(256)(128)(2,1)S(1)} %get-tuple-element.4), channel_id=1, source_target_pairs={{0,1},{1,2},{2,3},{3,4},{4,5},{5,6},{6,7},{7,8},{8,9},{9,10},{10,1... | collective-permute-start | bytes 1544 | tf_op jit(solution)/shard_map/ppermute | solution.py:13
  27.6 9.8 %collective-permute-start.4 = (bf16[256]{0:T(256)(128)(2,1)S(1)}, bf16[256]{0:T(256)(128)(2,1)S(1)}, u32[]{:S(2)}, u32[]{:S(2)}) collective-permute-start(bf16[256]{0:T(256)(128)(2,1)S(1)} %get-tuple-element.4), channel_id=1, source_target_pairs={{0,256},{256,512},{512,768},{768,0},{1,257},{257,513},{513,769},{7... | collective-permute-start | bytes 1544 | tf_op jit(solution)/shard_map/ppermute | solution.py:13
  33.6 3.8 %collective-permute-start.2 = (bf16[256]{0:T(256)(128)(2,1)S(1)}, bf16[256]{0:T(256)(128)(2,1)S(1)}, u32[]{:S(2)}, u32[]{:S(2)}) collective-permute-start(bf16[256]{0:T(256)(128)(2,1)S(1)} %collective-permute-done), channel_id=1, source_target_pairs={{0,1},{1,2},{2,3},{3,4},{4,5},{5,6},{6,7},{7,8},{8,9},{9,10},{10,1... | collective-permute-start | bytes 1544 | tf_op jit(solution)/shard_map/ppermute | solution.py:13
  37.4 31.2 %collective-permute-start.3 = (bf16[256,1152]{1,0:T(8,128)(2,1)S(1)}, bf16[256,1152]{1,0:T(8,128)(2,1)S(1)}, u32[]{:S(2)}, u32[]{:S(2)}) collective-permute-start(bf16[256,1152]{1,0:T(8,128)(2,1)S(1)} %collective-permute-done.1), channel_id=1, source_target_pairs={{0,1},{1,2},{2,3},{3,4},{4,5},{5,6},{6,7},{7,8},{8,9},{9,10},{10,1... | collective-permute-start | bytes 1769480 | tf_op jit(solution)/shard_map/ppermute | solution.py:13
  59.6 75.9 %collective-permute-start.8 = (f32[256,1152]{1,0:T(8,128)S(1)}, f32[256,1152]{1,0:T(8,128)S(1)}, u32[]{:S(2)}, u32[]{:S(2)}) collective-permute-start(f32[256,1152]{1,0:T(8,128)S(1)} %convolution_multiply_fusion), channel_id=1, source_target_pairs={{0,768},{256,0},{512,256},{768,512},{1,769},{257,1},{513,257},{769... | collective-permute-start | bytes 3538952 | tf_op jit(solution)/shard_map/ppermute | solution.py:13
  66.7 68.8 %collective-permute-start.6 = (f32[256,1152]{1,0:T(8,128)S(1)}, f32[256,1152]{1,0:T(8,128)S(1)}, u32[]{:S(2)}, u32[]{:S(2)}) collective-permute-start(f32[256,1152]{1,0:T(8,128)S(1)} %convolution_multiply_fusion.2), channel_id=1, source_target_pairs={{0,255},{1,0},{2,1},{3,2},{4,3},{5,4},{6,5},{7,6},{8,7},{9,8},{10,... | collective-permute-start | bytes 3538952 | tf_op jit(solution)/shard_map/ppermute | solution.py:13
  69.1 2.3 %copy-start.1 = (bf16[256,1152]{1,0:T(8,128)(2,1)S(1)}, bf16[256,1152]{1,0:T(8,128)(2,1)}, u32[]{:S(2)}) copy-start(bf16[256,1152]{1,0:T(8,128)(2,1)} %param.5) | copy-start | bytes 1769476
  69.6 65.9 %collective-permute-start.7 = (f32[256,1152]{1,0:T(8,128)S(1)}, f32[256,1152]{1,0:T(8,128)S(1)}, u32[]{:S(2)}, u32[]{:S(2)}) collective-permute-start(f32[256,1152]{1,0:T(8,128)S(1)} %convolution_multiply_fusion.1), channel_id=1, source_target_pairs={{0,254},{1,255},{2,0},{3,1},{4,2},{5,3},{6,4},{7,5},{8,6},{9,7},{1... | collective-permute-start | bytes 3538952 | tf_op jit(solution)/shard_map/ppermute | solution.py:13
where the time goes:
time: 137 us
  starting transfers between devices  64.9 us (47%)
  waiting for transfers between devices  60.7 us (44%)
  matrix products  8.27 us (6%)
  other arithmetic  1.95 us (1%)
    ppermute x9, starting transfers between devices, passed_along(): return lax.ppermute(value, axis, pairs)  64.9 us
    ppermute x9, waiting for transfers between devices, passed_along(): return lax.ppermute(value, axis, pairs)  60.7 us
    dot_general x4, matrix products, signed_logits(): lax.dot_general(images, texts, (((1,), (1,)), ((), ())), preferred_elemen...  3.2 us
  transfers between devices with their start and end apart: 9, of which 1 were waited for; matrix products, arithmetic and copies ran while one was open for 7% of the time, Pallas kernels for 0%

commit v1 on v0

v1 whole, which is shorter than its diff:
```python
import functools

import jax
import jax.numpy as jnp
from jax import lax
from jax.experimental import pallas as pl
from jax.experimental.pallas import tpu as pltpu
from jax.sharding import PartitionSpec as P

logit_scale = 10.0
logit_bias = -3.0
MESH = pl.DeviceIdType.MESH
CHUNK = 128

OWN_T, OWN_I, FAR_T, FAR_I, NEAR_T, NEAR_I, CROSS_T, CROSS_I = range(8)


def kernel(n_group, n_blk, image, text, image_ids, text_ids, loss, image_grad, text_grad,
           slots, tags, column_tags, acc, loss_acc, send, recv, tag_send, tag_recv):
    g, b = lax.axis_index("group"), lax.axis_index("blk")
    rows = image.shape[0]
    chunks = rows // CHUNK
    core = lax.rem(b, 2)
    partner = (g, b + 1 - 2 * core)
    ahead, behind = (g, lax.rem(b + 2, n_blk)), (g, lax.rem(b + n_blk - 2, n_blk))
    above, below = (lax.rem(g + 1, n_group), b), (lax.rem(g + n_group - 1, n_group), b)

    barrier = pltpu.get_barrier_semaphore()
    others = (partner, ahead, behind, above, below)
    for other in others:
        pl.semaphore_signal(barrier, inc=1, device_id=other, device_id_type=MESH)

    def span(k):
        return pl.ds(k * CHUNK, CHUNK)

    def local(source, slot, k):
        return pltpu.make_async_copy(source.at[span(k)], slots.at[slot, span(k)], recv.at[slot, k])

    def remote(source, slot, k, device):
        return pltpu.make_async_remote_copy(
            source.at[span(k)], slots.at[slot, span(k)], send.at[slot, k], recv.at[slot, k],
            device_id=device, device_id_type=MESH)

    def remote_tag(source, slot, device):
        return pltpu.make_async_remote_copy(
            source, tags.at[slot], tag_send.at[slot], tag_recv.at[slot],
            device_id=device, device_id_type=MESH)

    for slot, source, ids in ((OWN_T, text, text_ids), (OWN_I, image, image_ids)):
        for k in range(chunks):
            local(source, slot, k).start()
        tags[slot] = ids[...]
    for side, ids in ((0, image_ids), (1, text_ids)):
        column_tags[side] = jnp.transpose(jnp.broadcast_to(ids[...], (CHUNK, rows)))
    acc[...] = jnp.zeros_like(acc)
    loss_acc[...] = jnp.zeros_like(loss_acc)
    pl.semaphore_wait(barrier, len(others))

    plan = ((FAR_T, text, text_ids, ahead), (FAR_I, image, image_ids, behind),
            (CROSS_T, text, text_ids, above), (CROSS_I, image, image_ids, below))
    for slot, source, ids, device in plan:
        remote_tag(ids, slot, device).start()
    for slot, source, ids, device in plan:
        for k in range(chunks):
            remote(source, slot, k, device).start()

    @pl.when(core == 0)
    def _():
        remote_tag(text_ids, NEAR_T, partner).start()
        for k in range(chunks):
            remote(text, NEAR_T, k, partner).start()

    @pl.when(core == 1)
    def _():
        remote_tag(image_ids, NEAR_I, partner).start()
        for k in range(chunks):
            remote(image, NEAR_I, k, partner).start()

    def score(side, slot, k):
        mine = slots[OWN_I if side == 0 else OWN_T]
        theirs = slots[slot, span(k)]
        scores = lax.dot_general(mine, theirs, (((1,), (1,)), ((), ())), preferred_element_type=jnp.float32)
        logits = logit_scale * scores + logit_bias
        matched = column_tags[side] == tags[slot, :, span(k)]
        signed = jnp.where(matched, -logits, logits)
        small = jnp.exp(-jnp.abs(signed))
        sigmoid = jnp.where(signed >= 0, 1.0, small) / (1.0 + small)
        if side == 0:
            loss_acc[...] += jnp.maximum(signed, 0.0) + jnp.log1p(small)
        slopes = jnp.where(matched, -sigmoid, sigmoid).astype(jnp.bfloat16)
        acc[side] += jnp.dot(slopes, theirs, preferred_element_type=jnp.float32)

    for k in range(chunks):
        local(text, OWN_T, k).wait()
        local(image, OWN_I, k).wait()
    for side, slot in ((0, OWN_T), (1, OWN_I)):
        for k in range(chunks):
            score(side, slot, k)
    remote_tag(text_ids, FAR_T, ahead).wait_recv()
    remote_tag(image_ids, FAR_I, behind).wait_recv()

    @pl.when(core == 0)
    def _():
        remote_tag(tags.at[FAR_I], NEAR_I, partner).start()

    @pl.when(core == 1)
    def _():
        remote_tag(tags.at[FAR_T], NEAR_T, partner).start()

    for k in range(chunks):
        for side, slot, source, device in ((0, FAR_T, text, ahead), (1, FAR_I, image, behind)):
            remote(source, slot, k, device).wait_recv()

            @pl.when(core == 1 - side)
            def _(side=side, slot=slot, k=k):
                remote(slots.at[slot], NEAR_T if side == 0 else NEAR_I, k, partner).start()

            score(side, slot, k)
    remote_tag(text_ids, NEAR_T, partner).wait_recv()
    remote_tag(image_ids, NEAR_I, partner).wait_recv()
    for k in range(chunks):
        for side, slot, source in ((0, NEAR_T, text), (1, NEAR_I, image)):
            remote(source, slot, k, partner).wait_recv()
            score(side, slot, k)
    remote_tag(text_ids, CROSS_T, above).wait_recv()
    remote_tag(image_ids, CROSS_I, below).wait_recv()
    for k in range(chunks):
        for side, slot, source, device in ((0, CROSS_T, text, above), (1, CROSS_I, image, below)):
            remote(source, slot, k, device).wait_recv()
            score(side, slot, k)

    image_grad[...] = (logit_scale * acc[0]).astype(image_grad.dtype)
    text_grad[...] = (logit_scale * acc[1]).astype(text_grad.dtype)
    total = jnp.sum(jnp.transpose(loss_acc[...]), axis=0, keepdims=True)
    loss[...] = total / (4 * rows)

    for slot, source, ids, device in plan + ((NEAR_T, text, text_ids, partner), (NEAR_I, image, image_ids, partner)):
        remote_tag(ids, slot, device).wait_send()
        for k in range(chunks):
            remote(source, slot, k, device).wait_send()


def per_device(n_group, n_blk, image_emb, text_emb, image_ids, text_ids):
    rows, width = image_emb.shape
    chunks = rows // CHUNK
    in_vmem = pl.BlockSpec(memory_space=pltpu.VMEM)
    in_place = pl.BlockSpec(memory_space=pl.ANY)
    loss, image_grad, text_grad = pl.pallas_call(
        functools.partial(kernel, n_group, n_blk),
        out_shape=(
            jax.ShapeDtypeStruct((1, rows), jnp.float32),
            jax.ShapeDtypeStruct((rows, width), jnp.bfloat16),
            jax.ShapeDtypeStruct((rows, width), jnp.bfloat16),
        ),
        in_specs=[in_place, in_place, in_vmem, in_vmem],
        out_specs=(in_vmem, in_vmem, in_vmem),
        scratch_shapes=[
            pltpu.VMEM((8, rows, width), jnp.bfloat16),
            pltpu.VMEM((8, 1, rows), jnp.int32),
            pltpu.VMEM((2, rows, CHUNK), jnp.int32),
            pltpu.VMEM((2, rows, width), jnp.float32),
            pltpu.VMEM((rows, CHUNK), jnp.float32),
            pltpu.SemaphoreType.DMA((8, chunks)),
            pltpu.SemaphoreType.DMA((8, chunks)),
            pltpu.SemaphoreType.DMA((8,)),
            pltpu.SemaphoreType.DMA((8,)),
        ],
        compiler_params=pltpu.CompilerParams(collective_id=0, has_side_effects=True, vmem_limit_bytes=60 * 2**20),
        cost_estimate=pl.CostEstimate(flops=2 * 16 * rows * rows * width, bytes_accessed=8 * rows * width, transcendentals=0),
    )(image_emb, text_emb, image_ids.reshape(1, rows), text_ids.reshape(1, rows))
    return loss.reshape(rows), image_grad, text_grad


def solution(mesh):
    sizes = dict(mesh.shape)
    vector, matrix = P(("group", "blk")), P(("group", "blk"), None)
    return jax.shard_map(
        functools.partial(per_device, sizes["group"], sizes["blk"]), mesh=mesh,
        in_specs=(matrix, matrix, vector, vector), out_specs=(vector, matrix, matrix), check_vma=False)
```

time: 137 us -> 65.3 us (0.48)
  the two profiles are of different devices: /device:TPU:799 before, /device:TPU:32 now
where the time goes in v1:
time: 65.3 us; the launch traced here: 65.1 us
  Pallas kernels  60.5 us (93%)
  local copies, waits for them, and re-layouts  4.03 us (6%)
    pallas_call x1, Pallas kernels, per_device(): pl.pallas_call(functools.partial(kernel, n_group, n_blk), out_shape=(jax....  60.5 us
    unnamed x7, local copies, waits for them, and re-layouts  4.03 us

profile of v1, /device:TPU:32, one launch (start us, length us, event | category | flops | bytes accessed | tf_op | source)
XLA Modules:
  0.0 65.1 jit_solution(5256807048865429185)
XLA Ops:
  0.6 60.5 %shard_map.67 = (f32[1,256]{1,0:T(1,128)}, bf16[256,1152]{1,0:T(8,128)(2,1)}, bf16[256,1152]{1,0:T(8,128)(2,1)}) custom-call(bf16[256,1152]{1,0:T(8,128)(2,1)} %image.1, bf16[256,1152]{1,0:T(8,128)(2,1)} %text.1, s32[1,256]{1,0:T(1,128)} %bitcast.4, s32[1,256]{1,0:T(1,128)} %bitcast.5), custom_call_target="tpu_custom_call" | custom-call | flops 2415919104 | bytes 2359296 | tf_op jit(solution)/shard_map/pallas_call | solution.py:148
  61.1 0.0 copy-start.1
  61.1 0.7 %copy-done.1 = f32[1,256]{1,0:T(1,128)S(1)} copy-done((f32[1,256]{1,0:T(1,128)S(1)}, f32[1,256]{1,0:T(1,128)}, u32[]{:S(2)}) %copy-start.1) | copy-done | bytes 1048
  61.8 0.6 copy.10
  62.3 0.0 copy-start
  62.3 2.0 %copy.11 = bf16[256,1152]{1,0:T(8,128)(2,1)} copy(bf16[256,1152]{1,0:T(8,128)(2,1)} %get-tuple-element.13) | data formatting | bytes 1179648
  64.3 0.0 copy-done
  64.3 0.8 %copy.12 = bf16[256,1152]{1,0:T(8,128)(2,1)} copy(bf16[256,1152]{1,0:T(8,128)(2,1)S(1)} %copy-done) | data formatting | bytes 1179648
Async XLA Ops:
  61.1 0.7 %copy-start.1 = (f32[1,256]{1,0:T(1,128)S(1)}, f32[1,256]{1,0:T(1,128)}, u32[]{:S(2)}) copy-start(f32[1,256]{1,0:T(1,128)} %get-tuple-element.6) | copy-start | bytes 3076
  62.3 2.0 %copy-start = (bf16[256,1152]{1,0:T(8,128)(2,1)S(1)}, bf16[256,1152]{1,0:T(8,128)(2,1)}, u32[]{:S(2)}) copy-start(bf16[256,1152]{1,0:T(8,128)(2,1)} %get-tuple-element.14) | copy-start | bytes 1769476

commit v2 on v1

--- a/solution.py
+++ b/solution.py
@@ -11,24 +11,84 @@
 logit_bias = -3.0
 MESH = pl.DeviceIdType.MESH
 CHUNK = 128
+COLUMNS = 8
+PIECES = 4
 
 OWN_T, OWN_I, FAR_T, FAR_I, NEAR_T, NEAR_I, CROSS_T, CROSS_I = range(8)
+A_PARTNER, A_AHEAD, A_BEHIND, A_ABOVE, A_BELOW, A_DEST_T, A_DEST_I = range(7)
 
 
 def kernel(n_group, n_blk, image, text, image_ids, text_ids, loss, image_grad, text_grad,
-           slots, tags, column_tags, acc, loss_acc, send, recv, tag_send, tag_recv):
+           slots, relay, tags, column_tags, acc, loss_acc,
+           send, recv, tag_send, tag_recv, relay_send, relay_recv, answer, answer_t, answer_i):
     g, b = lax.axis_index("group"), lax.axis_index("blk")
     rows = image.shape[0]
     chunks = rows // CHUNK
-    core = lax.rem(b, 2)
+    part = rows // COLUMNS
+    per_chunk = CHUNK // part
+    depth = n_blk // (4 * COLUMNS)
+    core, x = lax.rem(b, 2), lax.rem(b // 2, COLUMNS)
+    low_y, z = lax.rem(b // (2 * COLUMNS), 2), b // (4 * COLUMNS)
+    last = COLUMNS - 1
+
+    def at(z_, y_, x_):
+        return (g, z_ * (4 * COLUMNS) + y_ * (2 * COLUMNS) + x_ * 2 + core)
+
     partner = (g, b + 1 - 2 * core)
     ahead, behind = (g, lax.rem(b + 2, n_blk)), (g, lax.rem(b + n_blk - 2, n_blk))
     above, below = (lax.rem(g + 1, n_group), b), (lax.rem(g + n_group - 1, n_group), b)
 
+    def crossing(k):
+        return at(z, 1 - low_y, k)
+
+    source_t, source_i = at(z, 1 - low_y, last), at(z, 1 - low_y, 0)
+    dest_t = at(lax.rem(z + 1 - low_y, depth), low_y, 0)
+    dest_i = at(lax.rem(z + depth - low_y, depth), low_y, last)
+
+    def relay_t(k):
+        return at(lax.rem(z + depth - 1 + low_y, depth), low_y, k)
+
+    def relay_i(k):
+        return at(lax.rem(z + low_y, depth), low_y, k)
+
+    def order(device):
+        index = device[0] * n_blk + device[1]
+        return jnp.where(index == 0, n_group * n_blk, index)
+
+    me = order((g, b))
+
+    def lower(device):
+        return order(device) < me
+
+    first, final = x == 0, x == last
     barrier = pltpu.get_barrier_semaphore()
-    others = (partner, ahead, behind, above, below)
-    for other in others:
-        pl.semaphore_signal(barrier, inc=1, device_id=other, device_id_type=MESH)
+
+    def announce(device, when=True):
+        @pl.when(jnp.logical_and(when, me < order(device)))
+        def _():
+            pl.semaphore_signal(barrier, inc=1, device_id=device, device_id_type=MESH)
+
+    def reply(device, semaphore, when=True):
+        @pl.when(jnp.logical_and(when, lower(device)))
+        def _():
+            pl.semaphore_signal(semaphore, inc=1, device_id=device, device_id_type=MESH)
+
+    def hear(device, semaphore, when=True):
+        @pl.when(jnp.logical_and(when, me < order(device)))
+        def _():
+            pl.semaphore_wait(semaphore, 1)
+
+    count = jnp.int32(0)
+    for device, when in ((partner, True), (ahead, True), (behind, True), (above, True), (below, True),
+                         (source_t, x > 0), (source_i, x < last), (dest_t, x > 0), (dest_i, x < last)):
+        announce(device, when)
+        count += jnp.where(jnp.logical_and(when, lower(device)), 1, 0)
+    for k in range(COLUMNS):
+        for device, when in ((crossing(k), final if k > 0 else None), (crossing(k), first if k < last else None),
+                             (relay_t(k), first if k > 0 else None), (relay_i(k), final if k < last else None)):
+            if when is not None:
+                announce(device, when)
+                count += jnp.where(jnp.logical_and(when, lower(device)), 1, 0)
 
     def span(k):
         return pl.ds(k * CHUNK, CHUNK)
@@ -44,6 +104,24 @@
     def remote_tag(source, slot, device):
         return pltpu.make_async_remote_copy(
             source, tags.at[slot], tag_send.at[slot], tag_recv.at[slot],
+            device_id=device, device_id_type=MESH)
+
+    def direct_part(source, slot, k, device):
+        return pltpu.make_async_remote_copy(
+            source.at[pl.ds(k * part, part)], slots.at[slot, pl.ds(k * part, part)],
+            send.at[slot, k // per_chunk], recv.at[slot, k // per_chunk],
+            device_id=device, device_id_type=MESH)
+
+    def to_relay(source, side, k, device):
+        return pltpu.make_async_remote_copy(
+            source.at[pl.ds(k * part, part)], relay.at[side],
+            send.at[FAR_T + side, k // per_chunk], relay_recv.at[side],
+            device_id=device, device_id_type=MESH)
+
+    def from_relay(side, device):
+        return pltpu.make_async_remote_copy(
+            relay.at[side], slots.at[FAR_T + side, pl.ds(pl.multiple_of(x * part, part), part)],
+            relay_send.at[side], recv.at[FAR_T + side, x // per_chunk],
             device_id=device, device_id_type=MESH)
 
     for slot, source, ids in ((OWN_T, text, text_ids), (OWN_I, image, image_ids)):
@@ -54,15 +132,25 @@
         column_tags[side] = jnp.transpose(jnp.broadcast_to(ids[...], (CHUNK, rows)))
     acc[...] = jnp.zeros_like(acc)
     loss_acc[...] = jnp.zeros_like(loss_acc)
-    pl.semaphore_wait(barrier, len(others))
-
-    plan = ((FAR_T, text, text_ids, ahead), (FAR_I, image, image_ids, behind),
-            (CROSS_T, text, text_ids, above), (CROSS_I, image, image_ids, below))
-    for slot, source, ids, device in plan:
-        remote_tag(ids, slot, device).start()
-    for slot, source, ids, device in plan:
-        for k in range(chunks):
-            remote(source, slot, k, device).start()
+
+    @pl.when(count > 0)
+    def _():
+        pl.semaphore_wait(barrier, count)
+
+    reply(partner, answer.at[A_PARTNER])
+    reply(ahead, answer.at[A_BEHIND])
+    reply(behind, answer.at[A_AHEAD])
+    reply(above, answer.at[A_BELOW])
+    reply(below, answer.at[A_ABOVE])
+    reply(source_t, answer_t.at[x], x > 0)
+    reply(source_i, answer_i.at[x], x < last)
+    for k in range(COLUMNS):
+        if k > 0:
+            reply(relay_t(k), answer.at[A_DEST_T], first)
+        if k < last:
+            reply(relay_i(k), answer.at[A_DEST_I], final)
+
+    hear(partner, answer.at[A_PARTNER])
 
     @pl.when(core == 0)
     def _():
@@ -75,6 +163,58 @@
         remote_tag(image_ids, NEAR_I, partner).start()
         for k in range(chunks):
             remote(image, NEAR_I, k, partner).start()
+
+    @pl.when(final)
+    def _():
+        for k in range(1, COLUMNS):
+            hear(crossing(k), answer_t.at[k])
+            to_relay(text, 0, k, crossing(k)).start()
+
+    @pl.when(first)
+    def _():
+        for k in range(COLUMNS - 1):
+            hear(crossing(k), answer_i.at[k])
+            to_relay(image, 1, k, crossing(k)).start()
+
+    hear(above, answer.at[A_ABOVE])
+    remote_tag(text_ids, CROSS_T, above).start()
+    for k in range(chunks):
+        remote(text, CROSS_T, k, above).start()
+    hear(below, answer.at[A_BELOW])
+    remote_tag(image_ids, CROSS_I, below).start()
+    for k in range(chunks):
+        remote(image, CROSS_I, k, below).start()
+
+    hear(ahead, answer.at[A_AHEAD])
+    remote_tag(text_ids, FAR_T, ahead).start()
+
+    @pl.when(final)
+    def _():
+        direct_part(text, FAR_T, 0, ahead).start()
+
+    @pl.when(jnp.logical_not(final))
+    def _():
+        for k in range(chunks):
+            remote(text, FAR_T, k, ahead).start()
+
+    def send_behind():
+        hear(behind, answer.at[A_BEHIND])
+        remote_tag(image_ids, FAR_I, behind).start()
+
+        @pl.when(first)
+        def _():
+            direct_part(image, FAR_I, last, behind).start()
+
+        @pl.when(jnp.logical_not(first))
+        def _():
+            for k in range(chunks):
+                remote(image, FAR_I, k, behind).start()
+
+    def pass_on(side):
+        pltpu.make_async_copy(relay.at[side], relay.at[side], relay_recv.at[side]).wait()
+        device = dest_t if side == 0 else dest_i
+        hear(device, answer.at[A_DEST_T + side])
+        from_relay(side, device).start()
 
     def score(side, slot, k):
         mine = slots[OWN_I if side == 0 else OWN_T]
@@ -90,12 +230,32 @@
         slopes = jnp.where(matched, -sigmoid, sigmoid).astype(jnp.bfloat16)
         acc[side] += jnp.dot(slopes, theirs, preferred_element_type=jnp.float32)
 
+    late = b < 2
+    late_relay = jnp.logical_and(z == 0, low_y == 1)
+
+    @pl.when(jnp.logical_not(late))
+    def _():
+        send_behind()
+
     for k in range(chunks):
         local(text, OWN_T, k).wait()
         local(image, OWN_I, k).wait()
     for side, slot in ((0, OWN_T), (1, OWN_I)):
         for k in range(chunks):
             score(side, slot, k)
+
+    @pl.when(x > 0)
+    def _():
+        pass_on(0)
+
+    @pl.when(jnp.logical_and(x < last, jnp.logical_not(late_relay)))
+    def _():
+        pass_on(1)
+
+    @pl.when(late)
+    def _():
+        send_behind()
+
     remote_tag(text_ids, FAR_T, ahead).wait_recv()
     remote_tag(image_ids, FAR_I, behind).wait_recv()
 
@@ -116,6 +276,11 @@
                 remote(slots.at[slot], NEAR_T if side == 0 else NEAR_I, k, partner).start()
 
             score(side, slot, k)
+
+    @pl.when(jnp.logical_and(x < last, late_relay))
+    def _():
+        pass_on(1)
+
     remote_tag(text_ids, NEAR_T, partner).wait_recv()
     remote_tag(image_ids, NEAR_I, partner).wait_recv()
     for k in range(chunks):
@@ -134,28 +299,50 @@
     total = jnp.sum(jnp.transpose(loss_acc[...]), axis=0, keepdims=True)
     loss[...] = total / (4 * rows)
 
-    for slot, source, ids, device in plan + ((NEAR_T, text, text_ids, partner), (NEAR_I, image, image_ids, partner)):
+    for slot, source, ids, device in (
+            (FAR_T, text, text_ids, ahead), (FAR_I, image, image_ids, behind),
+            (CROSS_T, text, text_ids, above), (CROSS_I, image, image_ids, below),
+            (NEAR_T, text, text_ids, partner), (NEAR_I, image, image_ids, partner)):
         remote_tag(ids, slot, device).wait_send()
         for k in range(chunks):
             remote(source, slot, k, device).wait_send()
+
+    @pl.when(x > 0)
+    def _():
+        from_relay(0, dest_t).wait_send()
+
+    @pl.when(x < last)
+    def _():
+        from_relay(1, dest_i).wait_send()
+
+
+def write_out(loss, image_grad, text_grad, loss_out, image_out, text_out, done):
+    piece = image_grad.shape[0] // PIECES
+    copies = [pltpu.make_async_copy(loss, loss_out, done.at[2 * PIECES])]
+    for i, (source, target) in enumerate(((image_grad, image_out), (text_grad, text_out))):
+        for k in range(PIECES):
+            part = pl.ds(k * piece, piece)
+            copies.append(pltpu.make_async_copy(source.at[part], target.at[part], done.at[i * PIECES + k]))
+    for copy in copies:
+        copy.start()
+    for copy in copies:
+        copy.wait()
 
 
 def per_device(n_group, n_blk, image_emb, text_emb, image_ids, text_ids):
     rows, width = image_emb.shape
     chunks = rows // CHUNK
     in_vmem = pl.BlockSpec(memory_space=pltpu.VMEM)
-    in_place = pl.BlockSpec(memory_space=pl.ANY)
-    loss, image_grad, text_grad = pl.pallas_call(
+    in_hbm = pl.BlockSpec(memory_space=pltpu.HBM)
+    shapes = ((1, rows), jnp.float32), ((rows, width), jnp.bfloat16), ((rows, width), jnp.bfloat16)
+    results = pl.pallas_call(
         functools.partial(kernel, n_group, n_blk),
-        out_shape=(
-            jax.ShapeDtypeStruct((1, rows), jnp.float32),
-            jax.ShapeDtypeStruct((rows, width), jnp.bfloat16),
-            jax.ShapeDtypeStruct((rows, width), jnp.bfloat16),
-        ),
-        in_specs=[in_place, in_place, in_vmem, in_vmem],
+        out_shape=tuple(pltpu.VMEM(*s) for s in shapes),
+        in_specs=[in_hbm, in_hbm, in_vmem, in_vmem],
         out_specs=(in_vmem, in_vmem, in_vmem),
         scratch_shapes=[
             pltpu.VMEM((8, rows, width), jnp.bfloat16),
+            pltpu.VMEM((2, rows // COLUMNS, width), jnp.bfloat16),
             pltpu.VMEM((8, 1, rows), jnp.int32),
             pltpu.VMEM((2, rows, CHUNK), jnp.int32),
             pltpu.VMEM((2, rows, width), jnp.float32),
@@ -164,10 +351,23 @@
             pltpu.SemaphoreType.DMA((8, chunks)),
             pltpu.SemaphoreType.DMA((8,)),
             pltpu.SemaphoreType.DMA((8,)),
+            pltpu.SemaphoreType.DMA((2,)),
+            pltpu.SemaphoreType.DMA((2,)),
+            pltpu.SemaphoreType.REGULAR((7,)),
+            pltpu.SemaphoreType.REGULAR((COLUMNS,)),
+            pltpu.SemaphoreType.REGULAR((COLUMNS,)),
         ],
-        compiler_params=pltpu.CompilerParams(collective_id=0, has_side_effects=True, vmem_limit_bytes=60 * 2**20),
+        compiler_params=pltpu.CompilerParams(collective_id=0, has_side_effects=True, vmem_limit_bytes=56 * 2**20),
         cost_estimate=pl.CostEstimate(flops=2 * 16 * rows * rows * width, bytes_accessed=8 * rows * width, transcendentals=0),
     )(image_emb, text_emb, image_ids.reshape(1, rows), text_ids.reshape(1, rows))
+    loss, image_grad, text_grad = pl.pallas_call(
+        write_out,
+        out_shape=tuple(jax.ShapeDtypeStruct(*s) for s in shapes),
+        in_specs=[in_vmem] * 3,
+        out_specs=(in_hbm, in_hbm, in_hbm),
+        scratch_shapes=[pltpu.SemaphoreType.DMA((2 * PIECES + 1,))],
+        compiler_params=pltpu.CompilerParams(vmem_limit_bytes=4 * 2**20),
+    )(*results)
     return loss.reshape(rows), image_grad, text_grad
 
 

time: 65.3 us -> 60.1 us (0.920)
  the two profiles are of different devices: /device:TPU:32 before, /device:TPU:1 now
where the time goes in v2:
time: 60.1 us; the launch traced here: 59.9 us
  Pallas kernels  59.3 us (99%)
  between operations  0.64 us (1%)
    pallas_call x1, Pallas kernels, per_device(): pl.pallas_call(functools.partial(kernel, n_group, n_blk), out_shape=tuple...  58.2 us

profile of v2, /device:TPU:1, one launch (start us, length us, event | category | flops | bytes accessed | tf_op | source)
XLA Modules:
  0.0 59.9 jit_solution(17812167356815289970)
XLA Ops:
  0.6 58.2 %shard_map.67 = (f32[1,256]{1,0:T(1,128)S(1)}, bf16[256,1152]{1,0:T(8,128)(2,1)S(1)}, bf16[256,1152]{1,0:T(8,128)(2,1)S(1)}) custom-call(bf16[256,1152]{1,0:T(8,128)(2,1)} %image.1, bf16[256,1152]{1,0:T(8,128)(2,1)} %text.1, s32[1,256]{1,0:T(1,128)} %bitcast.3, s32[1,256]{1,0:T(1,128)} %bitcast.4), custom_call_target="tpu_custom_call" | custom-call | flops 2415919104 | bytes 2359296 | tf_op jit(solution)/shard_map/pallas_call | solution.py:338
  58.8 1.1 %shard_map.68 = (f32[1,256]{1,0:T(1,128)}, bf16[256,1152]{1,0:T(8,128)(2,1)}, bf16[256,1152]{1,0:T(8,128)(2,1)}) custom-call(f32[1,256]{1,0:T(1,128)S(1)} %get-tuple-element.9.loss, bf16[256,1152]{1,0:T(8,128)(2,1)S(1)} %get-tuple-element.10.image_grad, bf16[256,1152]{1,0:T(8,128)(2,1)S(1)} %get-tuple-element.11.text_grad), custom_call_target="tpu_custom_call" | custom-call | tf_op jit(solution)/shard_map/pallas_call | solution.py:363

commit v3 on v2

--- a/solution.py
+++ b/solution.py
@@ -129,7 +129,7 @@
             local(source, slot, k).start()
         tags[slot] = ids[...]
     for side, ids in ((0, image_ids), (1, text_ids)):
-        column_tags[side] = jnp.transpose(jnp.broadcast_to(ids[...], (CHUNK, rows)))
+        column_tags[side] = jnp.transpose(jnp.broadcast_to(ids[...], (rows, rows)))
     acc[...] = jnp.zeros_like(acc)
     loss_acc[...] = jnp.zeros_like(loss_acc)
 
@@ -150,20 +150,6 @@
         if k < last:
             reply(relay_i(k), answer.at[A_DEST_I], final)
 
-    hear(partner, answer.at[A_PARTNER])
-
-    @pl.when(core == 0)
-    def _():
-        remote_tag(text_ids, NEAR_T, partner).start()
-        for k in range(chunks):
-            remote(text, NEAR_T, k, partner).start()
-
-    @pl.when(core == 1)
-    def _():
-        remote_tag(image_ids, NEAR_I, partner).start()
-        for k in range(chunks):
-            remote(image, NEAR_I, k, partner).start()
-
     @pl.when(final)
     def _():
         for k in range(1, COLUMNS):
@@ -176,26 +162,34 @@
             hear(crossing(k), answer_i.at[k])
             to_relay(image, 1, k, crossing(k)).start()
 
-    hear(above, answer.at[A_ABOVE])
-    remote_tag(text_ids, CROSS_T, above).start()
-    for k in range(chunks):
-        remote(text, CROSS_T, k, above).start()
-    hear(below, answer.at[A_BELOW])
-    remote_tag(image_ids, CROSS_I, below).start()
-    for k in range(chunks):
-        remote(image, CROSS_I, k, below).start()
-
-    hear(ahead, answer.at[A_AHEAD])
-    remote_tag(text_ids, FAR_T, ahead).start()
-
-    @pl.when(final)
-    def _():
-        direct_part(text, FAR_T, 0, ahead).start()
-
-    @pl.when(jnp.logical_not(final))
-    def _():
-        for k in range(chunks):
-            remote(text, FAR_T, k, ahead).start()
+    def send_above():
+        hear(above, answer.at[A_ABOVE])
+        remote_tag(text_ids, CROSS_T, above).start()
+        remote(text, CROSS_T, 0, above).start()
+
+    def send_below():
+        hear(below, answer.at[A_BELOW])
+        remote_tag(image_ids, CROSS_I, below).start()
+        remote(image, CROSS_I, 0, below).start()
+
+    late_above = jnp.logical_and(b == 0, g == n_group - 1)
+    top = z == depth - 1
+    late_below = jnp.logical_or(jnp.logical_and(b == 0, g == 1), top)
+    late_behind = jnp.logical_or(b < 2, jnp.logical_and(b == 2, g == 0))
+    late_relay = jnp.logical_and(z == 0, low_y == 1)
+    pl.when(jnp.logical_not(late_above))(send_above)
+    pl.when(jnp.logical_not(late_below))(send_below)
+    def send_ahead():
+        hear(ahead, answer.at[A_AHEAD])
+        remote_tag(text_ids, FAR_T, ahead).start()
+
+        @pl.when(final)
+        def _():
+            direct_part(text, FAR_T, 0, ahead).start()
+
+        @pl.when(jnp.logical_not(final))
+        def _():
+            remote(text, FAR_T, 0, ahead).start()
 
     def send_behind():
         hear(behind, answer.at[A_BEHIND])
@@ -207,7 +201,19 @@
 
         @pl.when(jnp.logical_not(first))
         def _():
-            for k in range(chunks):
+            remote(image, FAR_I, 0, behind).start()
+
+    def send_rest():
+        for k in range(1, chunks):
+            remote(text, CROSS_T, k, above).start()
+            remote(image, CROSS_I, k, below).start()
+
+            @pl.when(jnp.logical_not(final))
+            def _(k=k):
+                remote(text, FAR_T, k, ahead).start()
+
+            @pl.when(jnp.logical_not(first))
+            def _(k=k):
                 remote(image, FAR_I, k, behind).start()
 
     def pass_on(side):
@@ -216,58 +222,91 @@
         hear(device, answer.at[A_DEST_T + side])
         from_relay(side, device).start()
 
-    def score(side, slot, k):
+    def score(side, slot, start, length):
         mine = slots[OWN_I if side == 0 else OWN_T]
-        theirs = slots[slot, span(k)]
+        theirs = slots[slot, pl.ds(start, length)]
         scores = lax.dot_general(mine, theirs, (((1,), (1,)), ((), ())), preferred_element_type=jnp.float32)
         logits = logit_scale * scores + logit_bias
-        matched = column_tags[side] == tags[slot, :, span(k)]
+        matched = column_tags[side, :, :length] == tags[slot, :, pl.ds(start, length)]
         signed = jnp.where(matched, -logits, logits)
         small = jnp.exp(-jnp.abs(signed))
         sigmoid = jnp.where(signed >= 0, 1.0, small) / (1.0 + small)
         if side == 0:
-            loss_acc[...] += jnp.maximum(signed, 0.0) + jnp.log1p(small)
+            terms = jnp.maximum(signed, 0.0) + jnp.log1p(small)
+            for k in range(length // CHUNK):
+                loss_acc[...] += terms[:, k * CHUNK:(k + 1) * CHUNK]
         slopes = jnp.where(matched, -sigmoid, sigmoid).astype(jnp.bfloat16)
         acc[side] += jnp.dot(slopes, theirs, preferred_element_type=jnp.float32)
 
-    late = b < 2
-    late_relay = jnp.logical_and(z == 0, low_y == 1)
-
-    @pl.when(jnp.logical_not(late))
-    def _():
-        send_behind()
+    send_ahead()
+    pl.when(jnp.logical_not(late_behind))(send_behind)
+    hear(partner, answer.at[A_PARTNER])
+
+    @pl.when(core == 0)
+    def _():
+        remote_tag(text_ids, NEAR_T, partner).start()
+        for k in range(chunks):
+            remote(text, NEAR_T, k, partner).start()
+
+    @pl.when(core == 1)
+    def _():
+        remote_tag(image_ids, NEAR_I, partner).start()
+        for k in range(chunks):
+            remote(image, NEAR_I, k, partner).start()
 
     for k in range(chunks):
         local(text, OWN_T, k).wait()
         local(image, OWN_I, k).wait()
-    for side, slot in ((0, OWN_T), (1, OWN_I)):
-        for k in range(chunks):
-            score(side, slot, k)
+    score(0, OWN_T, 0, rows)
+    score(1, OWN_I, 0, rows)
 
     @pl.when(x > 0)
     def _():
         pass_on(0)
 
+    pl.when(late_above)(send_above)
+    pl.when(late_below)(send_below)
+
     @pl.when(jnp.logical_and(x < last, jnp.logical_not(late_relay)))
     def _():
         pass_on(1)
 
-    @pl.when(late)
-    def _():
+    late_rest = late_behind
+    pl.when(jnp.logical_not(late_rest))(send_rest)
+
+    @pl.when(late_rest)
+    def _():
+        for k in range(1, chunks):
+            remote(text, CROSS_T, k, above).start()
+            remote(image, CROSS_I, k, below).start()
+
+            @pl.when(jnp.logical_not(final))
+            def _(k=k):
+                remote(text, FAR_T, k, ahead).start()
+
         send_behind()
 
-    remote_tag(text_ids, FAR_T, ahead).wait_recv()
-    remote_tag(image_ids, FAR_I, behind).wait_recv()
-
-    @pl.when(core == 0)
-    def _():
-        remote_tag(tags.at[FAR_I], NEAR_I, partner).start()
-
-    @pl.when(core == 1)
-    def _():
-        remote_tag(tags.at[FAR_T], NEAR_T, partner).start()
-
-    for k in range(chunks):
+        @pl.when(jnp.logical_not(first))
+        def _():
+            for k in range(1, chunks):
+                remote(image, FAR_I, k, behind).start()
+
+    def tags_far():
+        remote_tag(text_ids, FAR_T, ahead).wait_recv()
+        remote_tag(image_ids, FAR_I, behind).wait_recv()
+
+        @pl.when(core == 0)
+        def _():
+            remote_tag(tags.at[FAR_I], NEAR_I, partner).start()
+
+        @pl.when(core == 1)
+        def _():
+            remote_tag(tags.at[FAR_T], NEAR_T, partner).start()
+
+    remote_tag(text_ids, CROSS_T, above).wait_recv()
+    remote_tag(image_ids, CROSS_I, below).wait_recv()
+
+    def far(k):
         for side, slot, source, device in ((0, FAR_T, text, ahead), (1, FAR_I, image, behind)):
             remote(source, slot, k, device).wait_recv()
 
@@ -275,24 +314,43 @@
             def _(side=side, slot=slot, k=k):
                 remote(slots.at[slot], NEAR_T if side == 0 else NEAR_I, k, partner).start()
 
-            score(side, slot, k)
-
-    @pl.when(jnp.logical_and(x < last, late_relay))
-    def _():
-        pass_on(1)
-
-    remote_tag(text_ids, NEAR_T, partner).wait_recv()
-    remote_tag(image_ids, NEAR_I, partner).wait_recv()
-    for k in range(chunks):
-        for side, slot, source in ((0, NEAR_T, text), (1, NEAR_I, image)):
-            remote(source, slot, k, partner).wait_recv()
-            score(side, slot, k)
-    remote_tag(text_ids, CROSS_T, above).wait_recv()
-    remote_tag(image_ids, CROSS_I, below).wait_recv()
-    for k in range(chunks):
+            score(side, slot, k * CHUNK, CHUNK)
+
+    def cross(k):
         for side, slot, source, device in ((0, CROSS_T, text, above), (1, CROSS_I, image, below)):
             remote(source, slot, k, device).wait_recv()
-            score(side, slot, k)
+            score(side, slot, k * CHUNK, CHUNK)
+
+    def near():
+        remote_tag(text_ids, NEAR_T, partner).wait_recv()
+        remote_tag(image_ids, NEAR_I, partner).wait_recv()
+        for side, slot, source in ((0, NEAR_T, text), (1, NEAR_I, image)):
+            for k in range(chunks):
+                remote(source, slot, k, partner).wait_recv()
+            score(side, slot, 0, rows)
+
+    @pl.when(b < 2)
+    def _():
+        cross(0)
+        cross(1)
+        tags_far()
+        far(0)
+        far(1)
+        near()
+
+    @pl.when(b >= 2)
+    def _():
+        tags_far()
+        far(0)
+        cross(0)
+        far(1)
+
+        @pl.when(jnp.logical_and(x < last, late_relay))
+        def _():
+            pass_on(1)
+
+        near()
+        cross(1)
 
     image_grad[...] = (logit_scale * acc[0]).astype(image_grad.dtype)
     text_grad[...] = (logit_scale * acc[1]).astype(text_grad.dtype)
@@ -344,7 +402,7 @@
             pltpu.VMEM((8, rows, width), jnp.bfloat16),
             pltpu.VMEM((2, rows // COLUMNS, width), jnp.bfloat16),
             pltpu.VMEM((8, 1, rows), jnp.int32),
-            pltpu.VMEM((2, rows, CHUNK), jnp.int32),
+            pltpu.VMEM((2, rows, rows), jnp.int32),
             pltpu.VMEM((2, rows, width), jnp.float32),
             pltpu.VMEM((rows, CHUNK), jnp.float32),
             pltpu.SemaphoreType.DMA((8, chunks)),

time: 60.1 us -> 52.5 us (0.87)
  Pallas kernels: 59.3 us -> 51.7 us
    pallas_call x1, Pallas kernels: 58.2 us -> 50.6 us  [per_device(): pl.pallas_call(functools.partial(kernel, n_group, n_blk), out_shape=tuple...]
where the time goes in v3:
time: 52.5 us; the launch traced here: 52.4 us
  Pallas kernels  51.7 us (98%)
  between operations  0.64 us (1%)
    pallas_call x1, Pallas kernels, per_device(): pl.pallas_call(functools.partial(kernel, n_group, n_blk), out_shape=tuple...  50.6 us
    pallas_call x1, Pallas kernels, per_device(): pl.pallas_call(write_out, out_shape=tuple((jax.ShapeDtypeStruct(*s) for s...  1.09 us

profile of v3, /device:TPU:1, one launch (start us, length us, event | category | flops | bytes accessed | tf_op | source)
XLA Modules:
  0.0 52.4 jit_solution(7211630870608657351)
XLA Ops:
  0.6 50.6 %shard_map.67 = (f32[1,256]{1,0:T(1,128)S(1)}, bf16[256,1152]{1,0:T(8,128)(2,1)S(1)}, bf16[256,1152]{1,0:T(8,128)(2,1)S(1)}) custom-call(bf16[256,1152]{1,0:T(8,128)(2,1)} %image.1, bf16[256,1152]{1,0:T(8,128)(2,1)} %text.1, s32[1,256]{1,0:T(1,128)} %bitcast.3, s32[1,256]{1,0:T(1,128)} %bitcast.4), custom_call_target="tpu_custom_call" | custom-call | flops 2415919104 | bytes 2359296 | tf_op jit(solution)/shard_map/pallas_call | solution.py:396
  51.3 1.1 %shard_map.68 = (f32[1,256]{1,0:T(1,128)}, bf16[256,1152]{1,0:T(8,128)(2,1)}, bf16[256,1152]{1,0:T(8,128)(2,1)}) custom-call(f32[1,256]{1,0:T(1,128)S(1)} %get-tuple-element.9.loss, bf16[256,1152]{1,0:T(8,128)(2,1)S(1)} %get-tuple-element.10.image_grad, bf16[256,1152]{1,0:T(8,128)(2,1)S(1)} %get-tuple-element.11.text_grad), custom_call_target="tpu_custom_call" | custom-call | tf_op jit(solution)/shard_map/pallas_call | solution.py:421

commit v4 on v3

--- a/solution.py
+++ b/solution.py
@@ -12,6 +12,7 @@
 MESH = pl.DeviceIdType.MESH
 CHUNK = 128
 COLUMNS = 8
+EARLY = 192
 PIECES = 4
 
 OWN_T, OWN_I, FAR_T, FAR_I, NEAR_T, NEAR_I, CROSS_T, CROSS_I = range(8)
@@ -101,6 +102,20 @@
             source.at[span(k)], slots.at[slot, span(k)], send.at[slot, k], recv.at[slot, k],
             device_id=device, device_id_type=MESH)
 
+    def bulk(source, slot, device, early):
+        spans = []
+        for k in range(chunks):
+            low, high = max(k * CHUNK, 0 if early else EARLY), min((k + 1) * CHUNK, EARLY if early else rows)
+            if low < high:
+                spans.append((k, pl.ds(low, high - low)))
+        return [pltpu.make_async_remote_copy(
+            source.at[part_], slots.at[slot, part_], send.at[slot, k], recv.at[slot, k],
+            device_id=device, device_id_type=MESH) for k, part_ in spans]
+
+    def start(copies):
+        for copy in copies:
+            copy.start()
+
     def remote_tag(source, slot, device):
         return pltpu.make_async_remote_copy(
             source, tags.at[slot], tag_send.at[slot], tag_recv.at[slot],
@@ -165,12 +180,12 @@
     def send_above():
         hear(above, answer.at[A_ABOVE])
         remote_tag(text_ids, CROSS_T, above).start()
-        remote(text, CROSS_T, 0, above).start()
+        start(bulk(text, CROSS_T, above, True))
 
     def send_below():
         hear(below, answer.at[A_BELOW])
         remote_tag(image_ids, CROSS_I, below).start()
-        remote(image, CROSS_I, 0, below).start()
+        start(bulk(image, CROSS_I, below, True))
 
     late_above = jnp.logical_and(b == 0, g == n_group - 1)
     top = z == depth - 1
@@ -189,7 +204,7 @@
 
         @pl.when(jnp.logical_not(final))
         def _():
-            remote(text, FAR_T, 0, ahead).start()
+            start(bulk(text, FAR_T, ahead, True))
 
     def send_behind():
         hear(behind, answer.at[A_BEHIND])
@@ -201,20 +216,14 @@
 
         @pl.when(jnp.logical_not(first))
         def _():
-            remote(image, FAR_I, 0, behind).start()
-
-    def send_rest():
-        for k in range(1, chunks):
-            remote(text, CROSS_T, k, above).start()
-            remote(image, CROSS_I, k, below).start()
-
-            @pl.when(jnp.logical_not(final))
-            def _(k=k):
-                remote(text, FAR_T, k, ahead).start()
-
-            @pl.when(jnp.logical_not(first))
-            def _(k=k):
-                remote(image, FAR_I, k, behind).start()
+            start(bulk(image, FAR_I, behind, True))
+
+    def send_rest(with_behind=True):
+        start(bulk(text, CROSS_T, above, False))
+        start(bulk(image, CROSS_I, below, False))
+        pl.when(jnp.logical_not(final))(lambda: start(bulk(text, FAR_T, ahead, False)))
+        if with_behind:
+            pl.when(jnp.logical_not(first))(lambda: start(bulk(image, FAR_I, behind, False)))
 
     def pass_on(side):
         pltpu.make_async_copy(relay.at[side], relay.at[side], relay_recv.at[side]).wait()
@@ -260,97 +269,82 @@
     score(0, OWN_T, 0, rows)
     score(1, OWN_I, 0, rows)
 
+    pl.when(jnp.logical_and(top, low_y == 1))(send_below)
+
     @pl.when(x > 0)
     def _():
         pass_on(0)
 
     pl.when(late_above)(send_above)
-    pl.when(late_below)(send_below)
+    pl.when(jnp.logical_and(late_below, jnp.logical_not(jnp.logical_and(top, low_y == 1))))(send_below)
 
     @pl.when(jnp.logical_and(x < last, jnp.logical_not(late_relay)))
     def _():
         pass_on(1)
 
-    late_rest = late_behind
-    pl.when(jnp.logical_not(late_rest))(send_rest)
-
-    @pl.when(late_rest)
-    def _():
-        for k in range(1, chunks):
-            remote(text, CROSS_T, k, above).start()
-            remote(image, CROSS_I, k, below).start()
-
-            @pl.when(jnp.logical_not(final))
-            def _(k=k):
-                remote(text, FAR_T, k, ahead).start()
-
+    pl.when(jnp.logical_not(late_behind))(send_rest)
+
+    @pl.when(late_behind)
+    def _():
+        send_rest(False)
         send_behind()
-
-        @pl.when(jnp.logical_not(first))
-        def _():
-            for k in range(1, chunks):
-                remote(image, FAR_I, k, behind).start()
-
-    def tags_far():
-        remote_tag(text_ids, FAR_T, ahead).wait_recv()
-        remote_tag(image_ids, FAR_I, behind).wait_recv()
-
-        @pl.when(core == 0)
-        def _():
-            remote_tag(tags.at[FAR_I], NEAR_I, partner).start()
-
-        @pl.when(core == 1)
-        def _():
-            remote_tag(tags.at[FAR_T], NEAR_T, partner).start()
-
-    remote_tag(text_ids, CROSS_T, above).wait_recv()
-    remote_tag(image_ids, CROSS_I, below).wait_recv()
-
-    def far(k):
-        for side, slot, source, device in ((0, FAR_T, text, ahead), (1, FAR_I, image, behind)):
-            remote(source, slot, k, device).wait_recv()
-
-            @pl.when(core == 1 - side)
-            def _(side=side, slot=slot, k=k):
-                remote(slots.at[slot], NEAR_T if side == 0 else NEAR_I, k, partner).start()
-
-            score(side, slot, k * CHUNK, CHUNK)
-
-    def cross(k):
-        for side, slot, source, device in ((0, CROSS_T, text, above), (1, CROSS_I, image, below)):
-            remote(source, slot, k, device).wait_recv()
-            score(side, slot, k * CHUNK, CHUNK)
-
-    def near():
-        remote_tag(text_ids, NEAR_T, partner).wait_recv()
-        remote_tag(image_ids, NEAR_I, partner).wait_recv()
-        for side, slot, source in ((0, NEAR_T, text), (1, NEAR_I, image)):
-            for k in range(chunks):
-                remote(source, slot, k, partner).wait_recv()
-            score(side, slot, 0, rows)
+        pl.when(jnp.logical_not(first))(lambda: start(bulk(image, FAR_I, behind, False)))
+
+    def far(side, k):
+        slot, source, ids, device = ((FAR_T, text, text_ids, ahead), (FAR_I, image, image_ids, behind))[side]
+        twin = (NEAR_T, NEAR_I)[side]
+        if k == 0:
+            remote_tag(ids, slot, device).wait_recv()
+            pl.when(core == 1 - side)(lambda: remote_tag(tags.at[slot], twin, partner).start())
+        remote(source, slot, k, device).wait_recv()
+        pl.when(core == 1 - side)(lambda: remote(slots.at[slot], twin, k, partner).start())
+        score(side, slot, k * CHUNK, CHUNK)
+
+    def cross(side, k):
+        slot, source, ids, device = ((CROSS_T, text, text_ids, above), (CROSS_I, image, image_ids, below))[side]
+        if k == 0:
+            remote_tag(ids, slot, device).wait_recv()
+        remote(source, slot, k, device).wait_recv()
+        score(side, slot, k * CHUNK, CHUNK)
+
+    def near(side):
+        slot, source, ids = ((NEAR_T, text, text_ids), (NEAR_I, image, image_ids))[side]
+        remote_tag(ids, slot, partner).wait_recv()
+        for k in range(chunks):
+            remote(source, slot, k, partner).wait_recv()
+        score(side, slot, 0, rows)
 
     @pl.when(b < 2)
     def _():
-        cross(0)
-        cross(1)
-        tags_far()
-        far(0)
-        far(1)
-        near()
+        far(1, 0)
+        far(1, 1)
+        near(1)
+        cross(0, 0)
+        cross(1, 0)
+        cross(0, 1)
+        cross(1, 1)
+        pl.when(core == 1)(lambda: near(0))
+        far(0, 0)
+        far(0, 1)
+        pl.when(core == 0)(lambda: near(0))
 
     @pl.when(b >= 2)
     def _():
-        tags_far()
-        far(0)
-        cross(0)
-        far(1)
+        far(0, 0)
+        far(1, 0)
+        cross(0, 0)
+        cross(1, 0)
+        far(0, 1)
+        far(1, 1)
 
         @pl.when(jnp.logical_and(x < last, late_relay))
         def _():
             pass_on(1)
 
-        near()
-        cross(1)
+        near(0)
+        near(1)
+        cross(0, 1)
+        cross(1, 1)
 
     image_grad[...] = (logit_scale * acc[0]).astype(image_grad.dtype)
     text_grad[...] = (logit_scale * acc[1]).astype(text_grad.dtype)

time: 52.5 us -> 52.9 us (level)
  no operation moved by 1% of the time
where the time goes in v4:
time: 52.9 us; the launch traced here: 52.7 us
  Pallas kernels  52.1 us (98%)
  between operations  0.64 us (1%)
    pallas_call x1, Pallas kernels, per_device(): pl.pallas_call(functools.partial(kernel, n_group, n_blk), out_shape=tuple...  51 us
    pallas_call x1, Pallas kernels, per_device(): pl.pallas_call(write_out, out_shape=tuple((jax.ShapeDtypeStruct(*s) for s...  1.09 us

profile of v4, /device:TPU:1, one launch (start us, length us, event | category | flops | bytes accessed | tf_op | source)
XLA Modules:
  0.0 52.7 jit_solution(12317411462188793161)
XLA Ops:
  0.6 51.0 %shard_map.67 = (f32[1,256]{1,0:T(1,128)S(1)}, bf16[256,1152]{1,0:T(8,128)(2,1)S(1)}, bf16[256,1152]{1,0:T(8,128)(2,1)S(1)}) custom-call(bf16[256,1152]{1,0:T(8,128)(2,1)} %image.1, bf16[256,1152]{1,0:T(8,128)(2,1)} %text.1, s32[1,256]{1,0:T(1,128)} %bitcast.3, s32[1,256]{1,0:T(1,128)} %bitcast.4), custom_call_target="tpu_custom_call" | custom-call | flops 2415919104 | bytes 2359296 | tf_op jit(solution)/shard_map/pallas_call | solution.py:390
  51.6 1.1 %shard_map.68 = (f32[1,256]{1,0:T(1,128)}, bf16[256,1152]{1,0:T(8,128)(2,1)}, bf16[256,1152]{1,0:T(8,128)(2,1)}) custom-call(f32[1,256]{1,0:T(1,128)S(1)} %get-tuple-element.9.loss, bf16[256,1152]{1,0:T(8,128)(2,1)S(1)} %get-tuple-element.10.image_grad, bf16[256,1152]{1,0:T(8,128)(2,1)S(1)} %get-tuple-element.11.text_grad), custom_call_target="tpu_custom_call" | custom-call | tf_op jit(solution)/shard_map/pallas_call | solution.py:415

commit v5 on v4

--- a/solution.py
+++ b/solution.py
@@ -143,10 +143,6 @@
         for k in range(chunks):
             local(source, slot, k).start()
         tags[slot] = ids[...]
-    for side, ids in ((0, image_ids), (1, text_ids)):
-        column_tags[side] = jnp.transpose(jnp.broadcast_to(ids[...], (rows, rows)))
-    acc[...] = jnp.zeros_like(acc)
-    loss_acc[...] = jnp.zeros_like(loss_acc)
 
     @pl.when(count > 0)
     def _():
@@ -263,6 +259,10 @@
         for k in range(chunks):
             remote(image, NEAR_I, k, partner).start()
 
+    for side, ids in ((0, image_ids), (1, text_ids)):
+        column_tags[side] = jnp.transpose(jnp.broadcast_to(ids[...], (rows, rows)))
+    acc[...] = jnp.zeros_like(acc)
+    loss_acc[...] = jnp.zeros_like(loss_acc)
     for k in range(chunks):
         local(text, OWN_T, k).wait()
         local(image, OWN_I, k).wait()

time: 52.9 us -> 52.9 us (level)
  no operation moved by 1% of the time
where the time goes in v5:
time: 52.9 us; the launch traced here: 52.7 us
  Pallas kernels  52.1 us (98%)
  between operations  0.64 us (1%)
    pallas_call x1, Pallas kernels, per_device(): pl.pallas_call(functools.partial(kernel, n_group, n_blk), out_shape=tuple...  51 us
    pallas_call x1, Pallas kernels, per_device(): pl.pallas_call(write_out, out_shape=tuple((jax.ShapeDtypeStruct(*s) for s...  1.09 us

profile of v5, /device:TPU:1, one launch (start us, length us, event | category | flops | bytes accessed | tf_op | source)
XLA Modules:
  0.0 52.7 jit_solution(14514034546462994508)
XLA Ops:
  0.6 51.0 %shard_map.67 = (f32[1,256]{1,0:T(1,128)S(1)}, bf16[256,1152]{1,0:T(8,128)(2,1)S(1)}, bf16[256,1152]{1,0:T(8,128)(2,1)S(1)}) custom-call(bf16[256,1152]{1,0:T(8,128)(2,1)} %image.1, bf16[256,1152]{1,0:T(8,128)(2,1)} %text.1, s32[1,256]{1,0:T(1,128)} %bitcast.3, s32[1,256]{1,0:T(1,128)} %bitcast.4), custom_call_target="tpu_custom_call" | custom-call | flops 2415919104 | bytes 2359296 | tf_op jit(solution)/shard_map/pallas_call | solution.py:390
  51.6 1.1 %shard_map.68 = (f32[1,256]{1,0:T(1,128)}, bf16[256,1152]{1,0:T(8,128)(2,1)}, bf16[256,1152]{1,0:T(8,128)(2,1)}) custom-call(f32[1,256]{1,0:T(1,128)S(1)} %get-tuple-element.9.loss, bf16[256,1152]{1,0:T(8,128)(2,1)S(1)} %get-tuple-element.10.image_grad, bf16[256,1152]{1,0:T(8,128)(2,1)S(1)} %get-tuple-element.11.text_grad), custom_call_target="tpu_custom_call" | custom-call | tf_op jit(solution)/shard_map/pallas_call | solution.py:415
